TPU v7x, 512 devices: a whole 4x4x16 slice. The times are simulated.
512 devices in a mesh: row: 16 (over z), col: 16 (over x, y_hi, core), rep: 2 (over y_lo).
Axes of the slice: x: 4, y: 4 (y_hi: 2, y_lo: 2; y = y_hi * 2 + y_lo), z: 16, core: 2. Of those that a mesh axis runs over, the one named last changes fastest.
Arguments:
- tokens: bfloat16 [768, 8192], P(('col', 'rep'), 'row'), may hold values from -6 to 6
- cotangent: bfloat16 [768, 8192], P(('col', 'rep'), 'row'), may hold values from -6 to 6
- w1_blocks: bfloat16 [4096, 128, 128], P(('row', 'col')), may hold values from -0.125 to 0.125
- w1_index: int32 [4096, 2], P(('row', 'col')), may hold values from 0 to 15, as said below
- w2_blocks: bfloat16 [4096, 128, 128], P(('row', 'col')), may hold values from -0.0625 to 0.0625
- w2_index: int32 [4096, 2], P(('row', 'col')), may hold values from 0 to 15, as said below
Outputs:
- output: bfloat16 [768, 8192], P(('col', 'rep'), 'row')
- grad_tokens: bfloat16 [768, 8192], P(('col', 'rep'), 'row')
- grad_w1: float32 [4096, 128, 128], P(('row', 'col', 'rep'))
- grad_w2: float32 [4096, 128, 128], P(('row', 'col', 'rep'))
Inputs may be any that keep to these rules, and one draw needn't show every extreme that they name: `w1_index`: the 16 pairs (block row, block column) of one tile, entries t * 16 to t * 16 + 15, are distinct; block rows lie below 4, block columns below 16. `w2_index`: the 16 pairs (block row, block column) of one tile, entries t * 16 to t * 16 + 15, are distinct; block rows lie below 16, block columns below 4.
All inputs are finite; a program needn't handle non-finite values.
Results may differ from a plain program's by a relative error of at most 0.018.
Values may be sent and summed in bfloat16 or wider, within the bound.
A program may use at most 64 MiB of HBM per device.

v0:
```python
import jax
import jax.numpy as jnp
from jax import lax
from jax.sharding import PartitionSpec as P

FF = 32768


def rounded(values):
    return lax.optimization_barrier(values.astype(jnp.bfloat16)).astype(jnp.float32)


def gelu_tanh(values):
    return jax.nn.gelu(values, approximate=True)


def tile_product(panels, blocks, pattern, in_index, out_index, n_in, n_out):
    row_count = panels.shape[0]
    block_size = blocks.shape[-1]
    picked = panels.reshape(row_count, n_in, block_size)[:, in_index, :]
    products = jnp.einsum(pattern, picked, blocks, preferred_element_type=jnp.float32)
    onehot = (out_index[:, None] == jnp.arange(n_out, dtype=jnp.int32)[None, :]).astype(jnp.float32)
    result = jnp.einsum("tne,no->toe", products, onehot, precision=lax.Precision.HIGHEST)
    return result.reshape(row_count, n_out * block_size)


def block_products(left_panel, right_panel, left_index, right_index, n_left, n_right):
    block_size = left_panel.shape[-1] // n_left
    lead = left_panel.shape[:-1]
    left_picked = left_panel.reshape(lead + (n_left, block_size))[:, :, left_index, :]
    right_picked = right_panel.reshape(lead + (n_right, block_size))[:, :, right_index, :]
    return jnp.einsum(
        "ptnb,ptne->pnbe", left_picked, right_picked, preferred_element_type=jnp.float32
    )


def shards(tokens, cotangent, w1_blocks, w1_index, w2_blocks, w2_index):
    block_size = w1_blocks.shape[-1]
    tile_rows = tokens.shape[1] // block_size
    tile_cols = FF // lax.axis_size("col") // block_size
    local_tokens = tokens.shape[0]
    row_share = local_tokens * lax.axis_size("col") // lax.axis_size("row")

    def column_panel(shard_data):
        return lax.all_gather(shard_data, "col", axis=0, tiled=True)

    def row_panel(shard_data):
        return lax.all_gather(shard_data, "row", axis=0, tiled=True)

    def row_sum(panels, blocks, pattern, in_index, out_index, n_in, n_out):
        terms = tile_product(panels, blocks, pattern, in_index, out_index, n_in, n_out).astype(
            jnp.bfloat16
        )
        pieces = lax.axis_size("row")
        stacked = terms.reshape(pieces, row_share, terms.shape[-1])
        received = lax.all_to_all(stacked, "row", split_axis=0, concat_axis=0, tiled=True)
        return jnp.sum(received.astype(jnp.float32), axis=0)

    def column_sum(panels, blocks, pattern, in_index, out_index, n_in, n_out):
        return lax.psum_scatter(
            rounded(tile_product(panels, blocks, pattern, in_index, out_index, n_in, n_out)).astype(
                jnp.bfloat16
            ),
            "col",
            scatter_dimension=0,
            tiled=True,
        ).astype(jnp.float32)

    token_panel = column_panel(tokens)
    hidden = row_sum(
        token_panel, w1_blocks, "tnb,nbe->tne", w1_index[:, 0], w1_index[:, 1], tile_rows, tile_cols
    )
    activated = gelu_tanh(hidden).astype(jnp.bfloat16)
    act_panel = row_panel(activated)
    output = column_sum(
        act_panel, w2_blocks, "tnb,nbe->tne", w2_index[:, 0], w2_index[:, 1], tile_cols, tile_rows
    ).astype(jnp.bfloat16)
    grad_panel = column_panel(cotangent)
    grad_act = row_sum(
        grad_panel, w2_blocks, "tnb,neb->tne", w2_index[:, 1], w2_index[:, 0], tile_rows, tile_cols
    )
    grad_hidden = jax.vjp(gelu_tanh, hidden)[1](grad_act)[0].astype(jnp.bfloat16)
    grad_hidden_panel = row_panel(grad_hidden)
    grad_tokens = column_sum(
        grad_hidden_panel,
        w1_blocks,
        "tnb,neb->tne",
        w1_index[:, 1],
        w1_index[:, 0],
        tile_cols,
        tile_rows,
    ).astype(jnp.bfloat16)
    gathered = (
        lax.all_gather(token_panel, "rep", axis=0, tiled=True),
        lax.all_gather(grad_hidden_panel, "rep", axis=0, tiled=True),
        lax.all_gather(act_panel, "rep", axis=0, tiled=True),
        lax.all_gather(grad_panel, "rep", axis=0, tiled=True),
    )
    replicas = lax.axis_size("rep")
    token_all = gathered[0].reshape(replicas, -1, gathered[0].shape[-1])
    hidden_all = gathered[1].reshape(replicas, -1, gathered[1].shape[-1])
    act_all = gathered[2].reshape(replicas, -1, gathered[2].shape[-1])
    cot_all = gathered[3].reshape(replicas, -1, gathered[3].shape[-1])
    half_blocks = w1_index.shape[0] // replicas
    own_first = lax.axis_index("rep") * half_blocks
    own_w1 = lax.dynamic_slice_in_dim(w1_index, own_first, half_blocks, 0)
    own_w2 = lax.dynamic_slice_in_dim(w2_index, own_first, half_blocks, 0)
    grad_w1 = jnp.sum(
        rounded(
            block_products(token_all, hidden_all, own_w1[:, 0], own_w1[:, 1], tile_rows, tile_cols)
        ),
        axis=0,
    )
    grad_w2 = jnp.sum(
        rounded(block_products(act_all, cot_all, own_w2[:, 0], own_w2[:, 1], tile_cols, tile_rows)),
        axis=0,
    )
    return (output, grad_tokens, grad_w1, grad_w2)


def solution(mesh):
    return jax.shard_map(
        shards,
        mesh=mesh,
        in_specs=(
            P(("col", "rep"), "row"),
            P(("col", "rep"), "row"),
            P(("row", "col"), None, None),
            P(("row", "col"), None),
            P(("row", "col"), None, None),
            P(("row", "col"), None),
        ),
        out_specs=(
            P(("col", "rep"), "row"),
            P(("col", "rep"), "row"),
            P(("row", "col", "rep"), None, None),
            P(("row", "col", "rep"), None, None),
        ),
        check_vma=False,
    )
```

profile of v0, /device:TPU:1, one launch (start us, length us, event | category | flops | bytes accessed | tf_op | source)
XLA Modules:
  0.0 653.9 jit_solution(10544713906011116803)
XLA Ops:
  7.2 27.2 %all_gather.24 = bf16[384,512]{1,0:T(8,128)(2,1)S(1)} all-gather(bf16[24,512]{1,0:T(8,128)(2,1)} %param.6), channel_id=1, replica_groups=mesh['row'=16,'col'=16,'rep'=2] {'col'}, dimensions={0}, use_global_device_ids=true | all-gather | bytes 417792 | tf_op jit(solution)/shard_map/all_gather | solution.py:45
  34.9 0.9 gather_fusion
  36.5 3.4 fusion.27
  39.9 2.1 convert_element_type.76
  42.0 15.1 %all-to-all-start = ((bf16[16,24,2048]{2,1,0:T(8,128)(2,1)}), bf16[16,24,2048]{2,1,0:T(8,128)(2,1)S(1)}, u32[]{:S(2)}, u32[]{:S(2)}) async-start(bf16[16,24,2048]{2,1,0:T(8,128)(2,1)} %convert_element_type.76), calls=%async_computation | async-start | bytes 3145728 | tf_op jit(solution)/shard_map/all_to_all | solution.py:56
  57.1 20.4 %all_gather.26 = bf16[384,512]{1,0:T(8,128)(2,1)S(1)} all-gather(bf16[24,512]{1,0:T(8,128)(2,1)S(1)} %copy-done.5), channel_id=1, replica_groups=mesh['row'=16,'col'=16,'rep'=2] {'col'}, dimensions={0}, use_global_device_ids=true | all-gather | bytes 417792 | tf_op jit(solution)/shard_map/all_gather | solution.py:45
  77.5 0.9 copy.42
  78.4 1.2 copy.43
  79.6 1.9 gather_fusion.2
  81.5 2.0 convolution_bitcast_fusion.1
  83.5 4.6 fusion.24
  88.1 3.7 convert_element_type.84
  91.8 34.6 %all-to-all-done = bf16[16,24,2048]{2,1,0:T(8,128)(2,1)S(1)} async-done(((bf16[16,24,2048]{2,1,0:T(8,128)(2,1)}), bf16[16,24,2048]{2,1,0:T(8,128)(2,1)S(1)}, u32[]{:S(2)}, u32[]{:S(2)}) %all-to-all-start) | async-done | bytes 1572896 | tf_op jit(solution)/shard_map/all_to_all | solution.py:56
  126.4 11.3 %all-to-all-start.1 = ((bf16[16,24,2048]{2,1,0:T(8,128)(2,1)}), bf16[16,24,2048]{2,1,0:T(8,128)(2,1)}, u32[]{:S(2)}, u32[]{:S(2)}) async-start(bf16[16,24,2048]{2,1,0:T(8,128)(2,1)} %convert_element_type.84), calls=%async_computation.2 | async-start | bytes 3145728 | tf_op jit(solution)/shard_map/all_to_all | solution.py:56
  138.0 68.7 %all-to-all-done.1 = bf16[16,24,2048]{2,1,0:T(8,128)(2,1)} async-done(((bf16[16,24,2048]{2,1,0:T(8,128)(2,1)}), bf16[16,24,2048]{2,1,0:T(8,128)(2,1)}, u32[]{:S(2)}, u32[]{:S(2)}) %all-to-all-start.1) | async-done | bytes 1572896 | tf_op jit(solution)/shard_map/all_to_all | solution.py:56
  206.7 1.7 convert_reduce_fusion
  208.4 0.8 fusion.52
  210.0 57.9 %all-gather.7.cloned.1.call-done = bf16[384,2048]{1,0:T(8,128)(2,1)} async-done(((bf16[24,2048]{1,0:T(8,128)(2,1)}), bf16[384,2048]{1,0:T(8,128)(2,1)}) %all-gather.7.cloned.1.call-update) | async-done | bytes 1572880 | tf_op jit(solution)/shard_map/all_gather | solution.py:48
  268.0 71.9 %all-gather.5.cloned.1.call-done = bf16[384,2048]{1,0:T(8,128)(2,1)} async-done(((bf16[24,2048]{1,0:T(8,128)(2,1)}), bf16[384,2048]{1,0:T(8,128)(2,1)}) %all-gather.5.cloned.1.call-update) | async-done | bytes 1572880 | tf_op jit(solution)/shard_map/all_gather | solution.py:48
  340.0 7.7 %all_gather.28 = bf16[768,512]{1,0:T(8,128)(2,1)S(1)} all-gather(bf16[384,512]{1,0:T(8,128)(2,1)S(1)} %all_gather.24), channel_id=1, replica_groups=mesh['row'=16,'col'=16,'rep'=2] {'rep'}, dimensions={0}, use_global_device_ids=true | all-gather | bytes 1179648 | tf_op jit(solution)/shard_map/all_gather | solution.py:94
  348.0 9.0 %all_gather.31 = bf16[768,512]{1,0:T(8,128)(2,1)S(1)} all-gather(bf16[384,512]{1,0:T(8,128)(2,1)S(1)} %all_gather.26), channel_id=1, replica_groups=mesh['row'=16,'col'=16,'rep'=2] {'rep'}, dimensions={0}, use_global_device_ids=true | all-gather | bytes 1179648 | tf_op jit(solution)/shard_map/all_gather | solution.py:97
  357.4 1.9 gather_fusion.4
  359.3 2.0 gather_fusion.7
  361.3 1.9 copy.39
  363.2 1.6 copy.40
  364.9 2.4 gather_fusion.1
  367.9 2.9 fusion.40
  370.8 0.8 copy.103
  371.7 0.9 copy.45
  372.5 1.0 copy.46
  373.8 0.9 gather_fusion.3
  374.6 1.6 convolution_bitcast_fusion
  376.3 2.9 fusion.43
  379.2 0.8 copy.102
  380.1 23.8 %all-gather.9.cloned.1.call-done = bf16[768,2048]{1,0:T(8,128)(2,1)} async-done(((bf16[384,2048]{1,0:T(8,128)(2,1)}), bf16[768,2048]{1,0:T(8,128)(2,1)}) %all-gather.9.cloned.1.call-update) | async-done | bytes 3145744 | tf_op jit(solution)/shard_map/all_gather | solution.py:95
  403.8 2.9 copy.62
  406.7 0.8 copy.49
  407.5 1.9 gather_fusion.5
  409.4 3.3 fusion.30
  412.8 49.2 %all-gather.11.cloned.1.call-done = bf16[768,2048]{1,0:T(8,128)(2,1)} async-done(((bf16[384,2048]{1,0:T(8,128)(2,1)}), bf16[768,2048]{1,0:T(8,128)(2,1)}) %all-gather.11.cloned.1.call-update) | async-done | bytes 3145744 | tf_op jit(solution)/shard_map/all_gather | solution.py:96
  462.0 2.9 copy.63
  464.9 0.8 copy.52
  465.7 1.9 gather_fusion.6
  467.6 2.6 fusion.35
  470.3 0.9 convert_reduce_fusion.3
  471.2 0.9 convert_reduce_fusion.2
  472.0 82.4 %reduce-scatter.3.cloned.1.call-done = bf16[24,512]{1,0:T(8,128)(2,1)} async-done(((bf16[384,512]{1,0:T(8,128)(2,1)}), bf16[24,512]{1,0:T(8,128)(2,1)}) %reduce-scatter.3.cloned.1.call-update) | async-done | bytes 24592 | tf_op jit(solution)/shard_map/reduce_scatter | solution.py:60
  554.5 92.5 %reduce-scatter.5.cloned.1.call-done = bf16[24,512]{1,0:T(8,128)(2,1)} async-done(((bf16[384,512]{1,0:T(8,128)(2,1)}), bf16[24,512]{1,0:T(8,128)(2,1)}) %reduce-scatter.5.cloned.1.call-update) | async-done | bytes 24592 | tf_op jit(solution)/shard_map/reduce_scatter | solution.py:60
  (49 shorter events, 4.0 us)
Async XLA Ops:
  7.2 74.3 %copy-start = (bf16[16,128,128]{2,1,0:T(8,128)(2,1)S(1)}, bf16[16,128,128]{2,1,0:T(8,128)(2,1)}, u32[]{:S(2)}) copy-start(bf16[16,128,128]{2,1,0:T(8,128)(2,1)} %param.10) | copy-start | bytes 1572868
  7.2 27.7 %copy-start.7 = (s32[16,2]{0,1:T(2,128)S(1)}, s32[16,2]{0,1:T(2,128)}, u32[]{:S(2)}) copy-start(s32[16,2]{0,1:T(2,128)} %param.11) | copy-start | bytes 388
  7.2 27.7 %copy-start.6 = (s32[16,2]{0,1:T(2,128)S(1)}, s32[16,2]{0,1:T(2,128)}, u32[]{:S(2)}) copy-start(s32[16,2]{0,1:T(2,128)} %param.9) | copy-start | bytes 388
  34.9 1.0 copy-start.3
  42.0 15.1 %copy-start.5 = (bf16[24,512]{1,0:T(8,128)(2,1)S(1)}, bf16[24,512]{1,0:T(8,128)(2,1)}, u32[]{:S(2)}) copy-start(bf16[24,512]{1,0:T(8,128)(2,1)} %param.7) | copy-start | bytes 73732
  42.0 84.4 %all-to-all-start = ((bf16[16,24,2048]{2,1,0:T(8,128)(2,1)}), bf16[16,24,2048]{2,1,0:T(8,128)(2,1)S(1)}, u32[]{:S(2)}, u32[]{:S(2)}) async-start(bf16[16,24,2048]{2,1,0:T(8,128)(2,1)} %convert_element_type.76), calls=%async_computation | async-start | bytes 3145728 | tf_op jit(solution)/shard_map/all_to_all | solution.py:56
  126.4 80.3 %all-to-all-start.1 = ((bf16[16,24,2048]{2,1,0:T(8,128)(2,1)}), bf16[16,24,2048]{2,1,0:T(8,128)(2,1)}, u32[]{:S(2)}, u32[]{:S(2)}) async-start(bf16[16,24,2048]{2,1,0:T(8,128)(2,1)} %convert_element_type.84), calls=%async_computation.2 | async-start | bytes 3145728 | tf_op jit(solution)/shard_map/all_to_all | solution.py:56
  137.7 130.2 %all-gather.7.cloned.1.call-start = ((), (), s32[]{:S(2)}) async-start(), calls=%async_computation.6 | async-start | bytes 1671168 | tf_op jit(solution)/shard_map/all_gather | solution.py:48
  209.2 130.7 %all-gather.5.cloned.1.call-start = ((), (), s32[]{:S(2)}) async-start(), calls=%async_computation.4 | async-start | bytes 1671168 | tf_op jit(solution)/shard_map/all_gather | solution.py:48
  210.0 193.8 %all-gather.9.cloned.1.call-start = ((), (), s32[]{:S(2)}) async-start(), calls=%async_computation.8 | async-start | bytes 4718592 | tf_op jit(solution)/shard_map/all_gather | solution.py:95
  267.9 194.0 %all-gather.11.cloned.1.call-start = ((), (), s32[]{:S(2)}) async-start(), calls=%async_computation.9 | async-start | bytes 4718592 | tf_op jit(solution)/shard_map/all_gather | solution.py:96
  339.9 214.6 %reduce-scatter.3.cloned.1.call-start = ((), (), s32[]{:S(2)}) async-start(), calls=%async_computation.5 | async-start | bytes 417792 | tf_op jit(solution)/shard_map/reduce_scatter | solution.py:60
  367.9 3.8 copy-start.2
  373.5 273.5 %reduce-scatter.5.cloned.1.call-start = ((), (), s32[]{:S(2)}) async-start(), calls=%async_computation.7 | async-start | bytes 417792 | tf_op jit(solution)/shard_map/reduce_scatter | solution.py:60
  467.6 2.6 copy-start.4
  467.6 179.4 %copy-start.1 = (bf16[16,128,128]{2,1,0:T(8,128)(2,1)S(1)}, bf16[16,128,128]{2,1,0:T(8,128)(2,1)}, u32[]{:S(2)}) copy-start(bf16[16,128,128]{2,1,0:T(8,128)(2,1)} %param.10) | copy-start | bytes 1572868
Sparse Core Ops, SparseCore 0:
  209.3 58.5 all-gather.6
  270.6 69.2 all-gather.4
  342.0 61.7 all-gather.8
  405.8 56.1 all-gather.10
  467.0 87.4 reduce-scatter.2
  559.5 87.4 reduce-scatter.4
where the time goes:
time: 655 us; the launch traced here: 654 us
  waiting for transfers between devices  482 us (74%)
  blocking collectives  64.2 us (10%)
  local copies, waits for them, and re-layouts  37.4 us (6%)
  starting transfers between devices  27 us (4%)
  matrix products  24.5 us (4%)
  between operations  14.4 us (2%)
    reduce_scatter x2, waiting for transfers between devices, column_sum(): lax.psum_scatter(rounded(tile_product(panels, blocks, pattern, in_index,...  175 us
    all_gather x2, waiting for transfers between devices, row_panel(): return lax.all_gather(shard_data, 'row', axis=0, tiled=True)  130 us
    all_to_all x2, waiting for transfers between devices, row_sum(): lax.all_to_all(stacked, 'row', split_axis=0, concat_axis=0, tiled=True)  103 us
    all_gather x1, waiting for transfers between devices, shards(): lax.all_gather(act_panel, 'rep', axis=0, tiled=True)  49.2 us
    all_gather x2, blocking collectives, column_panel(): return lax.all_gather(shard_data, 'col', axis=0, tiled=True)  47.5 us
    all_to_all x2, starting transfers between devices, row_sum(): lax.all_to_all(stacked, 'row', split_axis=0, concat_axis=0, tiled=True)  26.4 us
    all_gather x1, waiting for transfers between devices, shards(): lax.all_gather(grad_hidden_panel, 'rep', axis=0, tiled=True)  23.8 us
    dot_general x4, matrix products, tile_product(): jnp.einsum('tne,no->toe', products, onehot, precision=lax.Precision.HIGHEST)  13.9 us
  transfers between devices with their start and end apart: 8, of which 8 were waited for; matrix products, arithmetic and copies ran while one was open for 9% of the time, Pallas kernels for 0%

commit v1 on v0

v1 whole, which is shorter than its diff:
```python
import functools
import math

import jax
import jax.numpy as jnp
from jax import lax
from jax.experimental import pallas as pl
from jax.experimental.pallas import tpu as pltpu
from jax.sharding import PartitionSpec as P

BLK = 128
SUBS = 2
LAG = 2
F32 = jnp.float32
BF16 = jnp.bfloat16
NN = (((1,), (0,)), ((), ()))
NT = (((1,), (1,)), ((), ()))
TN = (((0,), (0,)), ((), ()))
C0 = math.sqrt(2.0 / math.pi)
C1 = 0.044715


def mm(left, right, dims):
    return lax.dot_general(left, right, dims, preferred_element_type=F32)


def stack_blocks(wide, parts):
    return jnp.concatenate([wide[:, a * BLK : (a + 1) * BLK] for a in range(parts)], axis=0)


def widen_blocks(tall, parts):
    rows = tall.shape[0] // parts
    return jnp.concatenate([tall[a * rows : (a + 1) * rows, :] for a in range(parts)], axis=1)


def kernel(
    n_row, n_col, tile_rows, n_blocks, own_blocks, tok_dev,
    tok_ref, cot_ref, inv_ref, idx1_ref, idx2_ref, w1_hbm, w2_hbm,
    out_ref, gt_ref, gw1_ref, gw2_ref,
    w1v, w2v, w1d, w2d, xrecv, xp, xk, part, rs, hid, ag0, ag1, acc, ysend, yrecv, wsend, wown, wrecv,
    load_sem, x_send, x_recv, rs_send, rs_recv, ag_send, ag_recv, y_send, y_recv, w_send, w_recv,
):
    ag = (ag0, ag1)
    z = lax.axis_index("row")
    c = lax.axis_index("col")
    p = lax.axis_index("rep")
    up, down = lax.rem(z + 1, n_row), lax.rem(z + n_row - 1, n_row)
    nxt = (up, down)
    half = n_row // 2
    tokens = tok_dev * n_col
    sub_rows = tokens // SUBS
    fw = tile_rows * BLK

    loads = [
        pltpu.make_async_copy(w1_hbm, w1v.at[pl.ds(0, n_blocks)], load_sem.at[0]),
        pltpu.make_async_copy(w2_hbm, w2v.at[pl.ds(0, n_blocks)], load_sem.at[1]),
    ]
    for load in loads:
        load.start()

    barrier = pltpu.get_barrier_semaphore()

    def greet(off, carry):
        pl.semaphore_signal(barrier, inc=1, device_id={"col": lax.rem(c + off, n_col)})
        return carry

    lax.fori_loop(1, n_col, greet, 0)
    pl.semaphore_signal(barrier, inc=1, device_id={"row": up})
    pl.semaphore_signal(barrier, inc=1, device_id={"row": down})
    pl.semaphore_signal(barrier, inc=1, device_id={"rep": 1 - p})

    for x, ref in enumerate((tok_ref, cot_ref)):
        xrecv[x, c] = stack_blocks(ref[...].astype(F32), tile_rows).astype(BF16)
    pl.semaphore_wait(barrier, n_col - 1 + 3)

    def x_copy(x, off, slot):
        return pltpu.make_async_remote_copy(
            src_ref=xrecv.at[x, slot],
            dst_ref=xrecv.at[x, slot],
            send_sem=x_send.at[x, off],
            recv_sem=x_recv.at[x, off],
            device_id={"col": lax.rem(c + off, n_col)},
        )

    for x in range(2):

        def send_x(off, carry, x=x):
            x_copy(x, off, c).start()
            return carry

        lax.fori_loop(1, n_col, send_x, 0)

    zero_block = jnp.zeros((BLK, BLK), BF16)
    w1v[n_blocks] = zero_block
    w2v[n_blocks] = zero_block
    zeros_half = jnp.zeros((tokens // 2, BLK), BF16)
    for ph in range(2):
        for way in range(2):
            for s_half in range(2):
                is_long = (s_half == 0) == (way == 0)
                rs[ph, way, half if is_long else half - 1, pl.ds(s_half * (tokens // 2), tokens // 2)] = zeros_half
        acc[ph] = jnp.zeros((tokens, fw), F32)
    for load in loads:
        load.wait()

    def dense(j, carry):
        for a in range(tile_rows):
            w1d[j, a * BLK : (a + 1) * BLK, :] = w1v[inv_ref[0, a * n_row + j]]
            w2d[j, :, a * BLK : (a + 1) * BLK] = w2v[inv_ref[1, j * tile_rows + a]]
        return carry

    lax.fori_loop(0, n_row, dense, 0)

    def panel(x):
        def arrive(off, carry):
            x_copy(x, off, lax.rem(c + n_col - off, n_col)).wait_recv()
            return carry

        lax.fori_loop(1, n_col, arrive, 0)
        for m in range(n_col // 2):
            pair = [widen_blocks(xrecv[x, 2 * m + h].astype(F32), tile_rows) for h in range(2)]
            rows = jnp.concatenate(pair, axis=0).astype(BF16)
            span = pl.ds(m * 2 * tok_dev, 2 * tok_dev)
            xp[x, span] = rows
            for a in range(tile_rows):
                xk[x, a, span] = rows[:, a * BLK : (a + 1) * BLK]

    def toward(way, d):
        return lax.rem(z + d, n_row) if way == 0 else lax.rem(z + n_row - d, n_row)

    def long_way(way, s):
        return (s < SUBS // 2) == (way == 0)

    def sub(s):
        return pl.ds(s * sub_rows, sub_rows)

    def product(ph, j):
        if ph == 0:
            return mm(xp[0], w1d[j], NN)
        return mm(xp[1], w2d[j], NT)

    def rs_copy(ph, way, d, s):
        return pltpu.make_async_remote_copy(
            src_ref=rs.at[ph, way, d, sub(s)],
            dst_ref=rs.at[ph, way, d - 1, sub(s)],
            send_sem=rs_send.at[ph, way, d, s],
            recv_sem=rs_recv.at[ph, way, d - 1, s],
            device_id={"row": nxt[way]},
        )

    def rs_terms(ph, d):
        for way in range(2):
            part[ph, way] = product(ph, toward(way, d))

    def rs_pass(ph, d):
        for s in range(SUBS):
            for way in range(2):
                is_long = long_way(way, s)
                last = half if is_long else half - 1

                @pl.when(d <= last)
                def _(s=s, way=way, last=last):
                    @pl.when(d <= last - 1)
                    def _():
                        rs_copy(ph, way, d + 1, s).wait_recv()

                    total = part[ph, way, sub(s)] + rs[ph, way, d, sub(s)].astype(F32)
                    rs[ph, way, d, sub(s)] = total.astype(BF16)
                    rs_copy(ph, way, d, s).start()

    def rs_end(ph):
        part[ph, 0] = product(ph, z)
        for s in range(SUBS):
            for way in range(2):
                rs_copy(ph, way, 1, s).wait_recv()
            total = part[ph, 0, sub(s)] + rs[ph, 0, 0, sub(s)].astype(F32) + rs[ph, 1, 0, sub(s)].astype(F32)
            if ph == 0:
                hid[sub(s)] = total
                tanh = jnp.tanh(C0 * (total + C1 * (total * total * total)))
                value = 0.5 * total * (1.0 + tanh)
            else:
                v = hid[sub(s)]
                tanh = jnp.tanh(C0 * (v + C1 * (v * v * v)))
                slope = 0.5 * (1.0 + tanh) + 0.5 * v * (1.0 - tanh * tanh) * (C0 * (1.0 + 3.0 * C1 * (v * v)))
                value = total * slope
            ag[ph][z, sub(s)] = value.astype(BF16)

    def origin(way, t):
        return lax.rem(z + n_row - t, n_row) if way == 0 else lax.rem(z + t, n_row)

    def ag_copy(ph, way, j, t, s):
        return pltpu.make_async_remote_copy(
            src_ref=ag[ph].at[j, sub(s)],
            dst_ref=ag[ph].at[j, sub(s)],
            send_sem=ag_send.at[ph, way, t, s],
            recv_sem=ag_recv.at[ph, way, t, s],
            device_id={"row": nxt[way]},
        )

    def ag_pass(ph, t):
        for s in range(SUBS):
            for way in range(2):
                hops = half if long_way(way, s) else half - 1
                j = origin(way, t)

                @pl.when((t >= 1) & (t <= hops))
                def _(s=s, way=way, j=j):
                    ag_copy(ph, way, j, t - 1, s).wait_recv()

                @pl.when(t <= hops - 1)
                def _(s=s, way=way, j=j):
                    ag_copy(ph, way, j, t, s).start()

    def consume(ph, j):
        if ph == 0:
            acc[0] += mm(ag0[j], w2d[j], NN)
        else:
            acc[1] += mm(ag1[j], w1d[j], NT)

    def ag_use(ph, t):
        consume(ph, origin(0, t))

        @pl.when((t >= 1) & (t <= half - 1))
        def _():
            consume(ph, origin(1, t))

    def item(i, phases):
        for ph in phases:
            n = i - LAG * ph

            @pl.when(n < half)
            def _(ph=ph, n=n):
                rs_terms(ph, half - n)
                rs_pass(ph, half - n)

            @pl.when(n == half)
            def _(ph=ph, n=n):
                rs_end(ph)

            @pl.when(n > half)
            def _(ph=ph, n=n):
                ag_pass(ph, n - half - 1)

        for ph in phases:
            n = i - LAG * ph

            @pl.when((n > half) & (n <= 2 * half + 1))
            def _(ph=ph, n=n):
                ag_use(ph, n - half - 1)

    panel(0)

    def first(i, carry):
        item(i, (0,))
        return carry

    lax.fori_loop(0, LAG, first, 0)
    panel(1)

    def both(i, carry):
        item(i, (0, 1))
        return carry

    lax.fori_loop(LAG, 2 * half + 1 + LAG, both, 0)

    def y_copy(ph, off, src_slot, dst_slot):
        return pltpu.make_async_remote_copy(
            src_ref=ysend.at[ph, src_slot],
            dst_ref=yrecv.at[ph, dst_slot],
            send_sem=y_send.at[ph, off],
            recv_sem=y_recv.at[ph, off],
            device_id={"col": lax.rem(c + off, n_col)},
        )

    def packed(ph, at):
        rows = acc[ph, pl.ds(pl.multiple_of(at * tok_dev, 8), tok_dev), :]
        return stack_blocks(rows, tile_rows).astype(BF16)

    def send_terms(ph):
        def one(off, carry):
            at = lax.rem(c + off, n_col)
            ysend[ph, at] = packed(ph, at)
            y_copy(ph, off, at, c).start()
            return carry

        lax.fori_loop(1, n_col, one, 0)
        yrecv[ph, c] = packed(ph, c)

    def sum_terms(ph, ref):
        def one(off, carry):
            at = lax.rem(c + n_col - off, n_col)
            y_copy(ph, off, at, at).wait_recv()
            return carry + yrecv[ph, at].astype(F32)

        total = lax.fori_loop(1, n_col, one, yrecv[ph, c].astype(F32))
        ref[...] = widen_blocks(total, tile_rows).astype(BF16)

    def w_copy(ph, m):
        return pltpu.make_async_remote_copy(
            src_ref=wsend.at[ph, m],
            dst_ref=wrecv.at[ph, m],
            send_sem=w_send.at[ph, m],
            recv_sem=w_recv.at[ph, m],
            device_id={"rep": 1 - p},
        )

    def weight_block(ph, n):
        if ph == 0:
            return mm(ag0[idx2_ref[n, 0]], xk[1, idx2_ref[n, 1]], TN)
        return mm(xk[0, idx1_ref[n, 0]], ag1[idx1_ref[n, 1]], TN)

    def send_weights(ph):
        def one(m, carry):
            wsend[ph, m] = weight_block(ph, (1 - p) * own_blocks + m).astype(BF16)
            w_copy(ph, m).start()
            return carry

        lax.fori_loop(0, own_blocks, one, 0)

    def own_weights(ph):
        def one(m, carry):
            wown[ph, m] = weight_block(ph, p * own_blocks + m).astype(BF16)
            return carry

        lax.fori_loop(0, own_blocks, one, 0)

    def sum_weights(ph, ref):
        def one(m, carry):
            w_copy(ph, m).wait_recv()
            ref[m] = wown[ph, m].astype(F32) + wrecv[ph, m].astype(F32)
            return carry

        lax.fori_loop(0, own_blocks, one, 0)

    send_terms(0)
    send_weights(0)
    ag_pass(1, half)
    ag_use(1, half)
    send_weights(1)
    send_terms(1)
    own_weights(0)
    own_weights(1)
    sum_terms(0, out_ref)
    sum_weights(0, gw2_ref)
    sum_terms(1, gt_ref)
    sum_weights(1, gw1_ref)

    for ph in range(2):

        def sent_cols(off, carry, ph=ph):
            x_copy(ph, off, c).wait_send()
            y_copy(ph, off, c, c).wait_send()
            return carry

        lax.fori_loop(1, n_col, sent_cols, 0)

        def sent_weights(m, carry, ph=ph):
            w_copy(ph, m).wait_send()
            return carry

        lax.fori_loop(0, own_blocks, sent_weights, 0)
        for way in range(2):
            for s in range(SUBS):
                hops = half if long_way(way, s) else half - 1

                def sent_rows(t, carry, ph=ph, way=way, s=s):
                    rs_copy(ph, way, t + 1, s).wait_send()
                    ag_copy(ph, way, z, t, s).wait_send()
                    return carry

                lax.fori_loop(0, hops, sent_rows, 0)


def inverse(keys, slots):
    count = keys.shape[0]
    number = jnp.arange(count, dtype=jnp.int32)
    hit = keys[:, None] == jnp.arange(slots, dtype=jnp.int32)[None, :]
    return count + jnp.sum(jnp.where(hit, number[:, None] - count, 0), axis=0)


def shards(n_row, n_col, tokens, cotangent, w1_blocks, w1_index, w2_blocks, w2_index):
    tok_dev, fw = tokens.shape
    tile_rows = fw // BLK
    n_blocks = w1_blocks.shape[0]
    own_blocks = n_blocks // 2
    half = n_row // 2
    toks = tok_dev * n_col
    slots = n_row * tile_rows
    inv = jnp.stack(
        [
            inverse(w1_index[:, 0] * n_row + w1_index[:, 1], slots),
            inverse(w2_index[:, 0] * tile_rows + w2_index[:, 1], slots),
        ]
    )
    vmem = pl.BlockSpec(memory_space=pltpu.VMEM)
    smem = pl.BlockSpec(memory_space=pltpu.SMEM)
    hbm = pl.BlockSpec(memory_space=pl.ANY)
    dma = pltpu.SemaphoreType.DMA
    return pl.pallas_call(
        functools.partial(kernel, n_row, n_col, tile_rows, n_blocks, own_blocks, tok_dev),
        out_shape=(
            jax.ShapeDtypeStruct((tok_dev, fw), BF16),
            jax.ShapeDtypeStruct((tok_dev, fw), BF16),
            jax.ShapeDtypeStruct((own_blocks, BLK, BLK), F32),
            jax.ShapeDtypeStruct((own_blocks, BLK, BLK), F32),
        ),
        in_specs=[vmem, vmem, smem, smem, smem, hbm, hbm],
        out_specs=[vmem] * 4,
        scratch_shapes=[
            pltpu.VMEM((n_blocks + 1, BLK, BLK), BF16),
            pltpu.VMEM((n_blocks + 1, BLK, BLK), BF16),
            pltpu.VMEM((n_row, fw, BLK), BF16),
            pltpu.VMEM((n_row, BLK, fw), BF16),
            pltpu.VMEM((2, n_col, tok_dev * tile_rows, BLK), BF16),
            pltpu.VMEM((2, toks, fw), BF16),
            pltpu.VMEM((2, tile_rows, toks, BLK), BF16),
            pltpu.VMEM((2, 2, toks, BLK), F32),
            pltpu.VMEM((2, 2, half + 1, toks, BLK), BF16),
            pltpu.VMEM((toks, BLK), F32),
            pltpu.VMEM((n_row, toks, BLK), BF16),
            pltpu.VMEM((n_row, toks, BLK), BF16),
            pltpu.VMEM((2, toks, fw), F32),
            pltpu.VMEM((2, n_col, tok_dev * tile_rows, BLK), BF16),
            pltpu.VMEM((2, n_col, tok_dev * tile_rows, BLK), BF16),
            pltpu.VMEM((2, own_blocks, BLK, BLK), BF16),
            pltpu.VMEM((2, own_blocks, BLK, BLK), BF16),
            pltpu.VMEM((2, own_blocks, BLK, BLK), BF16),
            dma((2,)),
            dma((2, n_col)),
            dma((2, n_col)),
            dma((2, 2, half + 1, SUBS)),
            dma((2, 2, half, SUBS)),
            dma((2, 2, half, SUBS)),
            dma((2, 2, half, SUBS)),
            dma((2, n_col)),
            dma((2, n_col)),
            dma((2, own_blocks)),
            dma((2, own_blocks)),
        ],
        compiler_params=pltpu.CompilerParams(
            collective_id=0, has_side_effects=True, vmem_limit_bytes=44 * 1024 * 1024
        ),
        name="ffn",
    )(tokens, cotangent, inv, w1_index, w2_index, w1_blocks, w2_blocks)


def solution(mesh):
    return jax.shard_map(
        functools.partial(shards, mesh.shape["row"], mesh.shape["col"]),
        mesh=mesh,
        in_specs=(
            P(("col", "rep"), "row"),
            P(("col", "rep"), "row"),
            P(("row", "col"), None, None),
            P(("row", "col"), None),
            P(("row", "col"), None, None),
            P(("row", "col"), None),
        ),
        out_specs=(
            P(("col", "rep"), "row"),
            P(("col", "rep"), "row"),
            P(("row", "col", "rep"), None, None),
            P(("row", "col", "rep"), None, None),
        ),
        check_vma=False,
    )
```

time: 655 us -> 127 us (0.19)
  waiting for transfers between devices: 482 us -> 0 us
  Pallas kernels: 0 us -> 118 us
  blocking collectives: 64.2 us -> 0 us
  local copies, waits for them, and re-layouts: 37.4 us -> 6.47 us
  starting transfers between devices: 27 us -> 0 us
  matrix products: 24.5 us -> 0 us
  between operations: 14.4 us -> 0.67 us
    all_gather x4 -> x0, waiting for transfers between devices: 203 us -> none  [the longest x2 130 us: row_panel(): return lax.all_gather(shard_data, 'row', axis=0, tiled=True)]
    reduce_scatter x2 -> x0, waiting for transfers between devices: 175 us -> none  [column_sum(): lax.psum_scatter(rounded(tile_product(panels, blocks, pattern, in_index,...]
    pallas_call x0 -> x1, Pallas kernels: none -> 118 us  [shards(): pl.pallas_call(functools.partial(kernel, n_row, n_col, tile_rows, n_block...]
    all_to_all x2 -> x0, waiting for transfers between devices: 103 us -> none  [row_sum(): lax.all_to_all(stacked, 'row', split_axis=0, concat_axis=0, tiled=True)]
    all_gather x4 -> x0, blocking collectives: 64.2 us -> none  [the longest x2 47.5 us: column_panel(): return lax.all_gather(shard_data, 'col', axis=0, tiled=True)]
    all_to_all x2 -> x0, starting transfers between devices: 26.4 us -> none  [row_sum(): lax.all_to_all(stacked, 'row', split_axis=0, concat_axis=0, tiled=True)]
    dot_general x10 -> x0, matrix products: 24.5 us -> none  [the longest x4 13.9 us: tile_product(): jnp.einsum('tne,no->toe', products, onehot, precision=lax.Precision.HIGHEST)]
    gather x8 -> x0, local copies, waits for them, and re-layouts: 13.7 us -> none  [the longest x4 6.01 us: tile_product(): picked = panels.reshape(row_count, n_in, block_size)[:, in_index, :]]
  transfers between devices with their start and end apart: 8 -> 0, of which waited for: 8 -> 0; matrix products, arithmetic and copies ran while one was open for 9% -> 0% of each run, Pallas kernels for 0% -> 0%
where the time goes in v1:
time: 127 us; the launch traced here: 126 us
  Pallas kernels  118 us (93%)
  local copies, waits for them, and re-layouts  6.47 us (5%)
    pallas_call x1, Pallas kernels, shards(): pl.pallas_call(functools.partial(kernel, n_row, n_col, tile_rows, n_block...  118 us
    unnamed x16, local copies, waits for them, and re-layouts  6.47 us

profile of v1, /device:TPU:1, one launch (start us, length us, event | category | flops | bytes accessed | tf_op | source)
XLA Modules:
  0.0 126.3 jit_solution(9385918365404975667)
XLA Ops:
  0.6 0.0 copy-start.4
  0.6 0.0 copy-start.2
  0.7 0.8 add_bitcast_fusion.3
  1.4 0.0 copy-done.4
  1.4 0.1 select_reduce_fusion.1
  1.5 0.8 copy.12.idx1_ref
  2.3 0.1 copy.13.idx2_ref
  2.4 0.0 copy-done.2
  2.4 0.0 copy-start
  2.4 1.0 copy-done
  3.4 0.0 copy-start.1
  3.4 1.0 copy-done.1
  4.5 0.0 copy-start.3
  4.5 0.7 copy-done.3
  5.2 118.3 %ffn.1 = (bf16[24,512]{1,0:T(8,128)(2,1)S(1)}, bf16[24,512]{1,0:T(8,128)(2,1)S(1)}, f32[8,128,128]{2,1,0:T(8,128)S(1)}, f32[8,128,128]{2,1,0:T(8,128)S(1)}) custom-call(bf16[24,512]{1,0:T(8,128)(2,1)S(1)} %copy-done.2, bf16[24,512]{1,0:T(8,128)(2,1)S(1)} %copy-done.3, s32[2,64]{1,0:T(2,128)S(1)} %pad_add_fusion.inv_ref, s32[16,2]{1,0:T(8,128)S(1)} %copy.12.idx1_ref, ...), custom_call_target="tpu_custom_call" | custom-call | tf_op jit(solution)/shard_map/ffn/pallas_call | solution.py:399
  123.5 0.6 copy.18
  124.1 0.6 copy.19
  124.7 0.8 copy.20
  125.5 0.8 copy.21
  (4 shorter events, 0.0 us)
Async XLA Ops:
  0.6 0.8 copy-start.4
  0.6 1.7 %copy-start.2 = (bf16[24,512]{1,0:T(8,128)(2,1)S(1)}, bf16[24,512]{1,0:T(8,128)(2,1)}, u32[]{:S(2)}) copy-start(bf16[24,512]{1,0:T(8,128)(2,1)} %tok_ref.1) | copy-start | bytes 73732
  2.4 1.0 copy-start
  3.4 1.0 copy-start.1
  4.5 0.7 copy-start.3

commit v2 on v1

v2 whole, which is shorter than its diff:
```python
import functools
import math

import jax
import jax.numpy as jnp
from jax import lax
from jax.experimental import pallas as pl
from jax.experimental.pallas import tpu as pltpu
from jax.sharding import PartitionSpec as P

BLK = 128
SUBS = 2
LAG = 2
F32 = jnp.float32
BF16 = jnp.bfloat16
NN = (((1,), (0,)), ((), ()))
NT = (((1,), (1,)), ((), ()))
TN = (((0,), (0,)), ((), ()))
C0 = math.sqrt(2.0 / math.pi)
C1 = 0.044715


def mm(left, right, dims):
    return lax.dot_general(left, right, dims, preferred_element_type=F32)


def stack_blocks(wide, parts):
    return jnp.concatenate([wide[:, a * BLK : (a + 1) * BLK] for a in range(parts)], axis=0)


def widen_blocks(tall, parts):
    rows = tall.shape[0] // parts
    return jnp.concatenate([tall[a * rows : (a + 1) * rows, :] for a in range(parts)], axis=1)


def kernel(
    n_row, n_col, tile_rows, n_blocks, own_blocks, tok_dev,
    tok_ref, cot_ref, idx1_hbm, idx2_hbm, w1_hbm, w2_hbm,
    out_ref, gt_ref, gw1_ref, gw2_ref,
    idx1, idx2, w1v, w2v, w1d, w2d, xrecv, xp, xt, part, rs, hid, ag0, ag1, acc, g1d, g2d,
    yown, ys1, yr1, ys2, yr2, ys3, yr3, wsend, wrecv,
    load_sem, x_send, x_recv, rs_send, rs_recv, ag_send, ag_recv, y1_sem, y2_send, y2_recv, y3_sem, w_send, w_recv,
):
    ag = (ag0, ag1)
    z = lax.axis_index("row")
    c = lax.axis_index("col")
    p = lax.axis_index("rep")
    up, down = lax.rem(z + 1, n_row), lax.rem(z + n_row - 1, n_row)
    nxt = (up, down)
    half = n_row // 2
    tokens = tok_dev * n_col
    sub_rows = tokens // SUBS
    fw = tile_rows * BLK
    n_chip = n_col // 2
    n_x = n_col // 4
    col_bits = n_col.bit_length() - 1
    bits = [lax.rem(c // (1 << b), 2) for b in range(col_bits)]
    core, y_hi, x_at = bits[0], bits[1], c // 4

    def flip(q):
        return sum((1 - bits[b] if (q >> b) & 1 else bits[b]) * (1 << b) for b in range(col_bits))

    loads = [
        pltpu.make_async_copy(idx1_hbm, idx1, load_sem.at[0]),
        pltpu.make_async_copy(idx2_hbm, idx2, load_sem.at[1]),
        pltpu.make_async_copy(w1_hbm, w1v.at[pl.ds(0, n_blocks)], load_sem.at[2]),
        pltpu.make_async_copy(w2_hbm, w2v.at[pl.ds(0, n_blocks)], load_sem.at[3]),
    ]
    for load in loads:
        load.start()

    barrier = pltpu.get_barrier_semaphore()
    peers = [flip(q) for q in range(1, n_col)]
    for peer in peers:
        pl.semaphore_signal(barrier, inc=1, device_id={"col": peer})
    pl.semaphore_signal(barrier, inc=1, device_id={"row": up})
    pl.semaphore_signal(barrier, inc=1, device_id={"row": down})
    pl.semaphore_signal(barrier, inc=1, device_id={"rep": 1 - p})

    for x, ref in enumerate((tok_ref, cot_ref)):
        xrecv[x, c] = stack_blocks(ref[...].astype(F32), tile_rows).astype(BF16)
    pl.semaphore_wait(barrier, len(peers) + 3)

    far = [q for q in range(2, n_col, 2) if q & 2] + [q for q in range(2, n_col, 2) if not q & 2]

    def x_copy(x, q, slot):
        return pltpu.make_async_remote_copy(
            src_ref=xrecv.at[x, slot],
            dst_ref=xrecv.at[x, slot],
            send_sem=x_send.at[x, q],
            recv_sem=x_recv.at[x, q],
            device_id={"col": flip(q if x == 0 else (1 if q % 2 else q))},
        )

    def x_start(x):
        for q in (far + [1] if x else far + [q + 1 for q in far] + [1]):
            x_copy(x, q, c).start()

    def x_forward(x):
        for q in (list(reversed(far)) if x else []):
            x_copy(x, q, flip(q)).wait_recv()
            x_copy(x, q + 1, flip(q)).start()

    def panel(x):
        for q in range(1, n_col, 2 if x else 1):
            x_copy(x, q, flip(q)).wait_recv()
        for m in range(n_col // 2):
            pair = [widen_blocks(xrecv[x, 2 * m + h].astype(F32), tile_rows) for h in range(2)]
            xp[x, pl.ds(m * 2 * tok_dev, 2 * tok_dev)] = jnp.concatenate(pair, axis=0).astype(BF16)

    x_start(0)

    zero_block = jnp.zeros((BLK, BLK), BF16)
    w1v[n_blocks] = zero_block
    w2v[n_blocks] = zero_block
    zeros_half = jnp.zeros((tokens // 2, BLK), BF16)
    for ph in range(2):
        for way in range(2):
            for s_half in range(2):
                is_long = (s_half == 0) == (way == 0)
                rs[ph, way, half if is_long else half - 1, pl.ds(s_half * (tokens // 2), tokens // 2)] = zeros_half

    def holder(keys, slot):
        found = jnp.int32(n_blocks)
        for n, key in enumerate(keys):
            found = jnp.where(key == slot, jnp.int32(n), found)
        return found

    def dense1():
        loads[0].wait()
        loads[2].wait()
        keys = [idx1[0, n] * n_row + idx1[1, n] for n in range(n_blocks)]

        def one(j, carry):
            for a in range(tile_rows):
                w1d[j, a * BLK : (a + 1) * BLK, :] = w1v[holder(keys, a * n_row + j)]
            return carry

        lax.fori_loop(0, n_row, one, 0)

    def dense2():
        loads[1].wait()
        loads[3].wait()
        keys = [idx2[0, n] * tile_rows + idx2[1, n] for n in range(n_blocks)]

        def one(j, carry):
            for a in range(tile_rows):
                w2d[j, :, a * BLK : (a + 1) * BLK] = w2v[holder(keys, j * tile_rows + a)]
            return carry

        lax.fori_loop(0, n_row, one, 0)

    def toward(way, d):
        return lax.rem(z + d, n_row) if way == 0 else lax.rem(z + n_row - d, n_row)

    def long_way(way, s):
        return (s < SUBS // 2) == (way == 0)

    def sub(s):
        return pl.ds(s * sub_rows, sub_rows)

    def product(ph, j):
        if ph == 0:
            return mm(xp[0], w1d[j], NN)
        return mm(xp[1], w2d[j], NT)

    def rs_copy(ph, way, d, s):
        return pltpu.make_async_remote_copy(
            src_ref=rs.at[ph, way, d, sub(s)],
            dst_ref=rs.at[ph, way, d - 1, sub(s)],
            send_sem=rs_send.at[ph, way, d, s],
            recv_sem=rs_recv.at[ph, way, d - 1, s],
            device_id={"row": nxt[way]},
        )

    def rs_terms(ph, d):
        for way in range(2):
            part[ph, way] = product(ph, toward(way, d))

    def rs_pass(ph, d):
        for s in range(SUBS):
            for way in range(2):
                is_long = long_way(way, s)
                last = half if is_long else half - 1

                @pl.when(d <= last)
                def _(s=s, way=way, last=last):
                    @pl.when(d <= last - 1)
                    def _():
                        rs_copy(ph, way, d + 1, s).wait_recv()

                    total = part[ph, way, sub(s)] + rs[ph, way, d, sub(s)].astype(F32)
                    rs[ph, way, d, sub(s)] = total.astype(BF16)
                    rs_copy(ph, way, d, s).start()

    def rs_end(ph):
        part[ph, 0] = product(ph, z)
        for s in range(SUBS):
            for way in range(2):
                rs_copy(ph, way, 1, s).wait_recv()
            total = part[ph, 0, sub(s)] + rs[ph, 0, 0, sub(s)].astype(F32) + rs[ph, 1, 0, sub(s)].astype(F32)
            if ph == 0:
                hid[sub(s)] = total
                tanh = jnp.tanh(C0 * (total + C1 * (total * total * total)))
                value = 0.5 * total * (1.0 + tanh)
            else:
                v = hid[sub(s)]
                tanh = jnp.tanh(C0 * (v + C1 * (v * v * v)))
                slope = 0.5 * (1.0 + tanh) + 0.5 * v * (1.0 - tanh * tanh) * (C0 * (1.0 + 3.0 * C1 * (v * v)))
                value = total * slope
            ag[ph][z, sub(s)] = value.astype(BF16)

    def origin(way, t):
        return lax.rem(z + n_row - t, n_row) if way == 0 else lax.rem(z + t, n_row)

    def ag_copy(ph, way, j, t, s):
        return pltpu.make_async_remote_copy(
            src_ref=ag[ph].at[j, sub(s)],
            dst_ref=ag[ph].at[j, sub(s)],
            send_sem=ag_send.at[ph, way, t, s],
            recv_sem=ag_recv.at[ph, way, t, s],
            device_id={"row": nxt[way]},
        )

    def ag_pass(ph, t):
        for s in range(SUBS):
            for way in range(2):
                hops = half if long_way(way, s) else half - 1
                j = origin(way, t)

                @pl.when((t >= 1) & (t <= hops))
                def _(s=s, way=way, j=j):
                    ag_copy(ph, way, j, t - 1, s).wait_recv()

                @pl.when(t <= hops - 1)
                def _(s=s, way=way, j=j):
                    ag_copy(ph, way, j, t, s).start()

    def consume(ph, j):
        if ph == 0:
            acc[0] += mm(ag0[j], w2d[j], NN)
            grad = mm(ag0[j], xp[1], TN)
            for a in range(tile_rows):
                g2d[j, a] = grad[:, a * BLK : (a + 1) * BLK].astype(BF16)
        else:
            acc[1] += mm(ag1[j], w1d[j], NT)
            grad = mm(xt[...], ag1[j], NN)
            for a in range(tile_rows):
                g1d[j, a] = grad[a * BLK : (a + 1) * BLK, :].astype(BF16)

    def ag_use(ph, t):
        consume(ph, origin(0, t))

        @pl.when((t >= 1) & (t <= half - 1))
        def _():
            consume(ph, origin(1, t))

    def item(i, phases):
        for ph in phases:
            n = i - LAG * ph

            @pl.when(n < half)
            def _(ph=ph, n=n):
                rs_terms(ph, half - n)
                rs_pass(ph, half - n)

            @pl.when(n == half)
            def _(ph=ph, n=n):
                rs_end(ph)

            @pl.when(n > half)
            def _(ph=ph, n=n):
                ag_pass(ph, n - half - 1)

        for ph in phases:
            n = i - LAG * ph

            @pl.when((n > half) & (n <= 2 * half + 1))
            def _(ph=ph, n=n):
                ag_use(ph, n - half - 1)

    def packed(ph, at):
        rows = acc[ph, pl.ds(pl.multiple_of(at * tok_dev, 8), tok_dev), :]
        return stack_blocks(rows, tile_rows)

    def y1_copy(ph):
        return pltpu.make_async_remote_copy(
            src_ref=ys1.at[ph],
            dst_ref=yr1.at[ph],
            send_sem=y1_sem.at[0, ph],
            recv_sem=y1_sem.at[1, ph],
            device_id={"col": flip(1)},
        )

    def y2_copy(ph, dx):
        to = flip(4 * dx)
        return pltpu.make_async_remote_copy(
            src_ref=ys2.at[ph, pl.ds(2 * (to // 4), 2)],
            dst_ref=yr2.at[ph, dx - 1],
            send_sem=y2_send.at[ph, dx - 1],
            recv_sem=y2_recv.at[ph, dx - 1],
            device_id={"col": to},
        )

    def y3_copy(ph):
        return pltpu.make_async_remote_copy(
            src_ref=ys3.at[ph],
            dst_ref=yr3.at[ph],
            send_sem=y3_sem.at[0, ph],
            recv_sem=y3_sem.at[1, ph],
            device_id={"col": flip(2)},
        )

    def y1(ph):
        def one(i, carry):
            ys1[ph, i] = packed(ph, 2 * i + 1 - core).astype(BF16)
            return carry

        lax.fori_loop(0, n_chip, one, 0)
        y1_copy(ph).start()

        def own(i, carry):
            yown[ph, i] = packed(ph, 2 * i + core)
            return carry

        lax.fori_loop(0, n_chip, own, 0)

    def y2(ph):
        y1_copy(ph).wait_recv()

        def one(i, carry):
            total = yown[ph, i] + yr1[ph, i].astype(F32)
            yown[ph, i] = total
            ys2[ph, i] = total.astype(BF16)
            return carry

        lax.fori_loop(0, n_chip, one, 0)
        for dx in range(1, n_x):
            y2_copy(ph, dx).start()

    def y3(ph):
        for dx in range(1, n_x):
            y2_copy(ph, dx).wait_recv()

        def summed(at):
            total = yown[ph, 2 * x_at + at]
            for dx in range(1, n_x):
                total += yr2[ph, dx - 1, at].astype(F32)
            return total

        ys3[ph] = summed(1 - y_hi).astype(BF16)
        y3_copy(ph).start()
        yown[ph, 0] = summed(y_hi)

    def y4(ph, ref):
        y3_copy(ph).wait_recv()
        ref[...] = widen_blocks(yown[ph, 0] + yr3[ph].astype(F32), tile_rows).astype(BF16)

    def w_copy(ph, m):
        return pltpu.make_async_remote_copy(
            src_ref=wsend.at[ph, m],
            dst_ref=wrecv.at[ph, m],
            send_sem=w_send.at[ph, m],
            recv_sem=w_recv.at[ph, m],
            device_id={"rep": 1 - p},
        )

    def weight_block(ph, n):
        if ph == 0:
            return g2d[idx2[0, n], idx2[1, n]]
        return g1d[idx1[1, n], idx1[0, n]]

    def send_weights(ph):
        def one(m, carry):
            wsend[ph, m] = weight_block(ph, (1 - p) * own_blocks + m)
            w_copy(ph, m).start()
            return carry

        lax.fori_loop(0, own_blocks, one, 0)

    def sum_weights(ph, ref):
        def one(m, carry):
            w_copy(ph, m).wait_recv()
            ref[m] = weight_block(ph, p * own_blocks + m).astype(F32) + wrecv[ph, m].astype(F32)
            return carry

        lax.fori_loop(0, own_blocks, one, 0)

    dense1()
    x_forward(0)
    x_start(1)
    panel(0)
    item(0, (0,))
    x_forward(1)
    dense2()
    for ph in range(2):
        acc[ph] = jnp.zeros((tokens, fw), F32)
    xt[...] = jnp.transpose(xp[0])

    def first(i, carry):
        item(i, (0,))
        return carry

    lax.fori_loop(1, LAG, first, 0)
    panel(1)

    def both(i, carry):
        item(i, (0, 1))

        @pl.when(i == 2 * half + 1)
        def _():
            y1(0)
            send_weights(0)

        return carry

    lax.fori_loop(LAG, 2 * half + 1 + LAG, both, 0)
    y2(0)
    ag_pass(1, half)
    ag_use(1, half)
    y1(1)
    send_weights(1)
    y3(0)
    y2(1)
    y4(0, out_ref)
    sum_weights(0, gw2_ref)
    y3(1)
    sum_weights(1, gw1_ref)
    y4(1, gt_ref)

    for ph in range(2):
        for q in range(1, n_col):
            x_copy(ph, q, c).wait_send()
        y1_copy(ph).wait_send()
        for dx in range(1, n_x):
            y2_copy(ph, dx).wait_send()
        y3_copy(ph).wait_send()

        def sent_weights(m, carry, ph=ph):
            w_copy(ph, m).wait_send()
            return carry

        lax.fori_loop(0, own_blocks, sent_weights, 0)
        for way in range(2):
            for s in range(SUBS):
                hops = half if long_way(way, s) else half - 1

                def sent_rows(t, carry, ph=ph, way=way, s=s):
                    rs_copy(ph, way, t + 1, s).wait_send()
                    ag_copy(ph, way, z, t, s).wait_send()
                    return carry

                lax.fori_loop(0, hops, sent_rows, 0)


def shards(n_row, n_col, tokens, cotangent, w1_blocks, w1_index, w2_blocks, w2_index):
    tok_dev, fw = tokens.shape
    tile_rows = fw // BLK
    n_blocks = w1_blocks.shape[0]
    own_blocks = n_blocks // 2
    half = n_row // 2
    toks = tok_dev * n_col
    n_chip = n_col // 2
    n_x = n_col // 4
    piece = (tok_dev * tile_rows, BLK)
    vmem = pl.BlockSpec(memory_space=pltpu.VMEM)
    hbm = pl.BlockSpec(memory_space=pltpu.HBM)
    dma = pltpu.SemaphoreType.DMA
    shapes = (
        pltpu.VMEM((tok_dev, fw), BF16),
        pltpu.VMEM((tok_dev, fw), BF16),
        pltpu.VMEM((own_blocks, BLK, BLK), F32),
        pltpu.VMEM((own_blocks, BLK, BLK), F32),
    )
    operands = [
        pltpu.with_memory_space_constraint(array, pltpu.HBM)
        for array in (tokens, cotangent, w1_index.T, w2_index.T, w1_blocks, w2_blocks)
    ]
    return pl.pallas_call(
        functools.partial(kernel, n_row, n_col, tile_rows, n_blocks, own_blocks, tok_dev),
        out_shape=shapes,
        in_specs=[vmem, vmem, hbm, hbm, hbm, hbm],
        out_specs=[vmem] * 4,
        scratch_shapes=[
            pltpu.SMEM((2, n_blocks), jnp.int32),
            pltpu.SMEM((2, n_blocks), jnp.int32),
            pltpu.VMEM((n_blocks + 1, BLK, BLK), BF16),
            pltpu.VMEM((n_blocks + 1, BLK, BLK), BF16),
            pltpu.VMEM((n_row, fw, BLK), BF16),
            pltpu.VMEM((n_row, BLK, fw), BF16),
            pltpu.VMEM((2, n_col) + piece, BF16),
            pltpu.VMEM((2, toks, fw), BF16),
            pltpu.VMEM((fw, toks), BF16),
            pltpu.VMEM((2, 2, toks, BLK), F32),
            pltpu.VMEM((2, 2, half + 1, toks, BLK), BF16),
            pltpu.VMEM((toks, BLK), F32),
            pltpu.VMEM((n_row, toks, BLK), BF16),
            pltpu.VMEM((n_row, toks, BLK), BF16),
            pltpu.VMEM((2, toks, fw), F32),
            pltpu.VMEM((n_row, tile_rows, BLK, BLK), BF16),
            pltpu.VMEM((n_row, tile_rows, BLK, BLK), BF16),
            pltpu.VMEM((2, n_chip) + piece, F32),
            pltpu.VMEM((2, n_chip) + piece, BF16),
            pltpu.VMEM((2, n_chip) + piece, BF16),
            pltpu.VMEM((2, n_chip) + piece, BF16),
            pltpu.VMEM((2, max(n_x - 1, 1), 2) + piece, BF16),
            pltpu.VMEM((2,) + piece, BF16),
            pltpu.VMEM((2,) + piece, BF16),
            pltpu.VMEM((2, own_blocks, BLK, BLK), BF16),
            pltpu.VMEM((2, own_blocks, BLK, BLK), BF16),
            dma((4,)),
            dma((2, n_col)),
            dma((2, n_col)),
            dma((2, 2, half + 1, SUBS)),
            dma((2, 2, half, SUBS)),
            dma((2, 2, half, SUBS)),
            dma((2, 2, half, SUBS)),
            dma((2, 2)),
            dma((2, max(n_x - 1, 1))),
            dma((2, max(n_x - 1, 1))),
            dma((2, 2)),
            dma((2, own_blocks)),
            dma((2, own_blocks)),
        ],
        compiler_params=pltpu.CompilerParams(
            collective_id=0, has_side_effects=True, vmem_limit_bytes=44 * 1024 * 1024
        ),
        name="ffn",
    )(*operands)


def solution(mesh):
    return jax.shard_map(
        functools.partial(shards, mesh.shape["row"], mesh.shape["col"]),
        mesh=mesh,
        in_specs=(
            P(("col", "rep"), "row"),
            P(("col", "rep"), "row"),
            P(("row", "col"), None, None),
            P(("row", "col"), None),
            P(("row", "col"), None, None),
            P(("row", "col"), None),
        ),
        out_specs=(
            P(("col", "rep"), "row"),
            P(("col", "rep"), "row"),
            P(("row", "col", "rep"), None, None),
            P(("row", "col", "rep"), None, None),
        ),
        check_vma=False,
    )
```

time: 127 us -> 116 us (0.913)
  Pallas kernels: 118 us -> 112 us
  local copies, waits for them, and re-layouts: 6.47 us -> 2.8 us
    pallas_call x1, Pallas kernels: 118 us -> 112 us  [shards(): pl.pallas_call(functools.partial(kernel, n_row, n_col, tile_rows, n_block...]
    unnamed x16 -> x4, local copies, waits for them, and re-layouts: 6.47 us -> 2.8 us
where the time goes in v2:
time: 116 us; the launch traced here: 115 us
  Pallas kernels  112 us (97%)
  local copies, waits for them, and re-layouts  2.8 us (2%)
    pallas_call x1, Pallas kernels, shards(): pl.pallas_call(functools.partial(kernel, n_row, n_col, tile_rows, n_block...  112 us
    unnamed x4, local copies, waits for them, and re-layouts  2.8 us

profile of v2, /device:TPU:1, one launch (start us, length us, event | category | flops | bytes accessed | tf_op | source)
XLA Modules:
  0.0 115.4 jit_solution(11547881034275099649)
XLA Ops:
  0.6 112.0 %ffn.1 = (bf16[24,512]{1,0:T(8,128)(2,1)S(1)}, bf16[24,512]{1,0:T(8,128)(2,1)S(1)}, f32[8,128,128]{2,1,0:T(8,128)S(1)}, f32[8,128,128]{2,1,0:T(8,128)S(1)}) custom-call(bf16[24,512]{1,0:T(8,128)(2,1)} %tok_ref.1, bf16[24,512]{1,0:T(8,128)(2,1)} %cot_ref.1, s32[2,16]{1,0:T(2,128)} %bitcast.2, s32[2,16]{1,0:T(2,128)} %bitcast.3, bf16[16,128,128]{2,1,0:T(8,128)(2,1)} %w1_hbm.1, ...), custom_call_target="tpu_custom_call" | custom-call | tf_op jit(solution)/shard_map/ffn/pallas_call | solution.py:479
  112.6 0.6 copy.14
  113.3 0.6 copy.15
  113.9 0.8 copy.16
  114.7 0.8 copy.17

commit v3 on v2

--- a/solution.py
+++ b/solution.py
@@ -38,8 +38,8 @@
     tok_ref, cot_ref, idx1_hbm, idx2_hbm, w1_hbm, w2_hbm,
     out_ref, gt_ref, gw1_ref, gw2_ref,
     idx1, idx2, w1v, w2v, w1d, w2d, xrecv, xp, xt, part, rs, hid, ag0, ag1, acc, g1d, g2d,
-    yown, ys1, yr1, ys2, yr2, ys3, yr3, wsend, wrecv,
-    load_sem, x_send, x_recv, rs_send, rs_recv, ag_send, ag_recv, y1_sem, y2_send, y2_recv, y3_sem, w_send, w_recv,
+    yown, ylast, ys1, yr1, ys2, yr2, ys3, yr3, wsend, wrecv,
+    load_sem, x_send, x_recv, rs_send, rs_recv, ag_send, ag_recv, y1_send, y1_recv, y2_send, y2_recv, y3_sem, w_send, w_recv,
 ):
     ag = (ag0, ag1)
     z = lax.axis_index("row")
@@ -51,14 +51,15 @@
     tokens = tok_dev * n_col
     sub_rows = tokens // SUBS
     fw = tile_rows * BLK
-    n_chip = n_col // 2
     n_x = n_col // 4
     col_bits = n_col.bit_length() - 1
     bits = [lax.rem(c // (1 << b), 2) for b in range(col_bits)]
-    core, y_hi, x_at = bits[0], bits[1], c // 4
+    core, y_hi = bits[0], bits[1]
 
     def flip(q):
         return sum((1 - bits[b] if (q >> b) & 1 else bits[b]) * (1 << b) for b in range(col_bits))
+
+    own_place = 2 * (c // 4) + core
 
     loads = [
         pltpu.make_async_copy(idx1_hbm, idx1, load_sem.at[0]),
@@ -78,35 +79,52 @@
     pl.semaphore_signal(barrier, inc=1, device_id={"rep": 1 - p})
 
     for x, ref in enumerate((tok_ref, cot_ref)):
-        xrecv[x, c] = stack_blocks(ref[...].astype(F32), tile_rows).astype(BF16)
+        xrecv[x, own_place] = stack_blocks(ref[...].astype(F32), tile_rows).astype(BF16)
     pl.semaphore_wait(barrier, len(peers) + 3)
 
-    far = [q for q in range(2, n_col, 2) if q & 2] + [q for q in range(2, n_col, 2) if not q & 2]
-
-    def x_copy(x, q, slot):
-        return pltpu.make_async_remote_copy(
-            src_ref=xrecv.at[x, slot],
-            dst_ref=xrecv.at[x, slot],
+    near = [q for q in range(1, n_col) if not q & 2]
+    far = [q for q in range(1, n_col) if q & 2]
+    even = [q for q in far + near if q % 2 == 0]
+
+    def place(q):
+        return (q >> 1 & 1) * (n_col // 2) + 2 * (flip(q) // 4) + (1 - core if q % 2 else core)
+
+    def x_copy(x, q, direct=True):
+        source = place(0) if direct else place(q)
+        return pltpu.make_async_remote_copy(
+            src_ref=xrecv.at[x, source],
+            dst_ref=xrecv.at[x, (q >> 1 & 1) * (n_col // 2) + place(0) if direct else place(q)],
             send_sem=x_send.at[x, q],
             recv_sem=x_recv.at[x, q],
             device_id={"col": flip(q if x == 0 else (1 if q % 2 else q))},
         )
 
+    def x_arrive(x, q):
+        x_copy(x, q, False).wait_recv()
+
     def x_start(x):
-        for q in (far + [1] if x else far + [q + 1 for q in far] + [1]):
-            x_copy(x, q, c).start()
+        for q in even + [1] if x else near + far:
+            x_copy(x, q).start()
 
     def x_forward(x):
-        for q in (list(reversed(far)) if x else []):
-            x_copy(x, q, flip(q)).wait_recv()
-            x_copy(x, q + 1, flip(q)).start()
-
-    def panel(x):
-        for q in range(1, n_col, 2 if x else 1):
-            x_copy(x, q, flip(q)).wait_recv()
-        for m in range(n_col // 2):
-            pair = [widen_blocks(xrecv[x, 2 * m + h].astype(F32), tile_rows) for h in range(2)]
-            xp[x, pl.ds(m * 2 * tok_dev, 2 * tok_dev)] = jnp.concatenate(pair, axis=0).astype(BF16)
+        for q in reversed(even):
+            x_arrive(x, q)
+            pltpu.make_async_remote_copy(
+                src_ref=xrecv.at[x, place(q)],
+                dst_ref=xrecv.at[x, place(q)],
+                send_sem=x_send.at[x, q + 1],
+                recv_sem=x_recv.at[x, q + 1],
+                device_id={"col": flip(1)},
+            ).start()
+
+    def panel(x, part_no):
+        for q in (near, far)[part_no]:
+            if x == 0 or q % 2:
+                x_arrive(x, q)
+        for m in range(n_col // 4):
+            at = part_no * (n_col // 2) + 2 * m
+            pair = [widen_blocks(xrecv[x, at + h].astype(F32), tile_rows) for h in range(2)]
+            xp[x, pl.ds(at * tok_dev, 2 * tok_dev)] = jnp.concatenate(pair, axis=0).astype(BF16)
 
     x_start(0)
 
@@ -159,10 +177,10 @@
     def sub(s):
         return pl.ds(s * sub_rows, sub_rows)
 
-    def product(ph, j):
+    def product(ph, j, rows):
         if ph == 0:
-            return mm(xp[0], w1d[j], NN)
-        return mm(xp[1], w2d[j], NT)
+            return mm(xp[0, rows], w1d[j], NN)
+        return mm(xp[1, rows], w2d[j], NT)
 
     def rs_copy(ph, way, d, s):
         return pltpu.make_async_remote_copy(
@@ -173,19 +191,23 @@
             device_id={"row": nxt[way]},
         )
 
-    def rs_terms(ph, d):
-        for way in range(2):
-            part[ph, way] = product(ph, toward(way, d))
-
-    def rs_pass(ph, d):
-        for s in range(SUBS):
+    def rs_terms(ph, n, subs):
+        for s in subs:
             for way in range(2):
-                is_long = long_way(way, s)
-                last = half if is_long else half - 1
-
-                @pl.when(d <= last)
-                def _(s=s, way=way, last=last):
-                    @pl.when(d <= last - 1)
+                d = (half if long_way(way, s) else half - 1) - n
+
+                @pl.when(d >= 1)
+                def _(s=s, way=way, d=d):
+                    part[ph, way, sub(s)] = product(ph, toward(way, d), sub(s))
+
+    def rs_pass(ph, n, subs):
+        for s in subs:
+            for way in range(2):
+                d = (half if long_way(way, s) else half - 1) - n
+
+                @pl.when(d >= 1)
+                def _(s=s, way=way, d=d):
+                    @pl.when(n >= 1)
                     def _():
                         rs_copy(ph, way, d + 1, s).wait_recv()
 
@@ -194,7 +216,8 @@
                     rs_copy(ph, way, d, s).start()
 
     def rs_end(ph):
-        part[ph, 0] = product(ph, z)
+        for s in range(SUBS):
+            part[ph, 0, sub(s)] = product(ph, z, sub(s))
         for s in range(SUBS):
             for way in range(2):
                 rs_copy(ph, way, 1, s).wait_recv()
@@ -209,6 +232,8 @@
                 slope = 0.5 * (1.0 + tanh) + 0.5 * v * (1.0 - tanh * tanh) * (C0 * (1.0 + 3.0 * C1 * (v * v)))
                 value = total * slope
             ag[ph][z, sub(s)] = value.astype(BF16)
+            for way in range(2):
+                ag_copy(ph, way, z, 0, s).start()
 
     def origin(way, t):
         return lax.rem(z + n_row - t, n_row) if way == 0 else lax.rem(z + t, n_row)
@@ -228,7 +253,7 @@
                 hops = half if long_way(way, s) else half - 1
                 j = origin(way, t)
 
-                @pl.when((t >= 1) & (t <= hops))
+                @pl.when(t <= hops)
                 def _(s=s, way=way, j=j):
                     ag_copy(ph, way, j, t - 1, s).wait_recv()
 
@@ -261,34 +286,35 @@
 
             @pl.when(n < half)
             def _(ph=ph, n=n):
-                rs_terms(ph, half - n)
-                rs_pass(ph, half - n)
+                rs_terms(ph, n, range(SUBS))
+                rs_pass(ph, n, range(SUBS))
 
             @pl.when(n == half)
-            def _(ph=ph, n=n):
+            def _(ph=ph):
                 rs_end(ph)
 
             @pl.when(n > half)
             def _(ph=ph, n=n):
-                ag_pass(ph, n - half - 1)
+                ag_pass(ph, n - half)
 
         for ph in phases:
             n = i - LAG * ph
 
-            @pl.when((n > half) & (n <= 2 * half + 1))
+            @pl.when((n >= half) & (n <= 2 * half))
             def _(ph=ph, n=n):
-                ag_use(ph, n - half - 1)
+                ag_use(ph, n - half)
 
     def packed(ph, at):
         rows = acc[ph, pl.ds(pl.multiple_of(at * tok_dev, 8), tok_dev), :]
         return stack_blocks(rows, tile_rows)
 
-    def y1_copy(ph):
-        return pltpu.make_async_remote_copy(
-            src_ref=ys1.at[ph],
-            dst_ref=yr1.at[ph],
-            send_sem=y1_sem.at[0, ph],
-            recv_sem=y1_sem.at[1, ph],
+    def y1_copy(ph, dx):
+        at = 2 * (flip(4 * dx) // 4)
+        return pltpu.make_async_remote_copy(
+            src_ref=ys1.at[ph, pl.ds(at, 2)],
+            dst_ref=yr1.at[ph, pl.ds(at, 2)],
+            send_sem=y1_send.at[ph, dx],
+            recv_sem=y1_recv.at[ph, dx],
             device_id={"col": flip(1)},
         )
 
@@ -311,50 +337,46 @@
             device_id={"col": flip(2)},
         )
 
+    x_order = sorted(range(n_x), key=lambda dx: (dx == 0, dx != 2))
+
     def y1(ph):
-        def one(i, carry):
-            ys1[ph, i] = packed(ph, 2 * i + 1 - core).astype(BF16)
-            return carry
-
-        lax.fori_loop(0, n_chip, one, 0)
-        y1_copy(ph).start()
-
-        def own(i, carry):
-            yown[ph, i] = packed(ph, 2 * i + core)
-            return carry
-
-        lax.fori_loop(0, n_chip, own, 0)
+        for dx in x_order:
+            at = 2 * (flip(4 * dx) // 4)
+            for y in range(2):
+                ys1[ph, at + y] = packed(ph, lax.rem(y + y_hi, 2) * (n_col // 2) + at + 1 - core).astype(BF16)
+            y1_copy(ph, dx).start()
 
     def y2(ph):
-        y1_copy(ph).wait_recv()
-
-        def one(i, carry):
-            total = yown[ph, i] + yr1[ph, i].astype(F32)
-            yown[ph, i] = total
-            ys2[ph, i] = total.astype(BF16)
-            return carry
-
-        lax.fori_loop(0, n_chip, one, 0)
-        for dx in range(1, n_x):
-            y2_copy(ph, dx).start()
+        for dx in x_order:
+            at = 2 * (flip(4 * dx) // 4)
+            own = [packed(ph, lax.rem(y + y_hi, 2) * (n_col // 2) + at + core) for y in range(2)]
+            y1_copy(ph, dx).wait_recv()
+            for y in range(2):
+                total = own[y] + yr1[ph, at + y].astype(F32)
+                if dx:
+                    ys2[ph, at + y] = total.astype(BF16)
+                else:
+                    yown[ph, y] = total
+            if dx:
+                y2_copy(ph, dx).start()
 
     def y3(ph):
         for dx in range(1, n_x):
             y2_copy(ph, dx).wait_recv()
 
         def summed(at):
-            total = yown[ph, 2 * x_at + at]
+            total = yown[ph, at]
             for dx in range(1, n_x):
                 total += yr2[ph, dx - 1, at].astype(F32)
             return total
 
         ys3[ph] = summed(1 - y_hi).astype(BF16)
         y3_copy(ph).start()
-        yown[ph, 0] = summed(y_hi)
+        ylast[ph] = summed(y_hi)
 
     def y4(ph, ref):
         y3_copy(ph).wait_recv()
-        ref[...] = widen_blocks(yown[ph, 0] + yr3[ph].astype(F32), tile_rows).astype(BF16)
+        ref[...] = widen_blocks(ylast[ph] + yr3[ph].astype(F32), tile_rows).astype(BF16)
 
     def w_copy(ph, m):
         return pltpu.make_async_remote_copy(
@@ -387,34 +409,36 @@
         lax.fori_loop(0, own_blocks, one, 0)
 
     dense1()
-    x_forward(0)
     x_start(1)
-    panel(0)
-    item(0, (0,))
-    x_forward(1)
+    for s in range(SUBS):
+        panel(0, s)
+        rs_terms(0, 0, (s,))
+        rs_pass(0, 0, (s,))
     dense2()
     for ph in range(2):
         acc[ph] = jnp.zeros((tokens, fw), F32)
-    xt[...] = jnp.transpose(xp[0])
 
     def first(i, carry):
         item(i, (0,))
         return carry
 
     lax.fori_loop(1, LAG, first, 0)
-    panel(1)
+    x_forward(1)
+    xt[...] = jnp.transpose(xp[0])
+    panel(1, 0)
+    panel(1, 1)
 
     def both(i, carry):
         item(i, (0, 1))
 
-        @pl.when(i == 2 * half + 1)
+        @pl.when(i == 2 * half)
         def _():
             y1(0)
             send_weights(0)
 
         return carry
 
-    lax.fori_loop(LAG, 2 * half + 1 + LAG, both, 0)
+    lax.fori_loop(LAG, 2 * half + LAG, both, 0)
     y2(0)
     ag_pass(1, half)
     ag_use(1, half)
@@ -430,8 +454,9 @@
 
     for ph in range(2):
         for q in range(1, n_col):
-            x_copy(ph, q, c).wait_send()
-        y1_copy(ph).wait_send()
+            x_copy(ph, q).wait_send()
+        for dx in range(n_x):
+            y1_copy(ph, dx).wait_send()
         for dx in range(1, n_x):
             y2_copy(ph, dx).wait_send()
         y3_copy(ph).wait_send()
@@ -499,7 +524,8 @@
             pltpu.VMEM((2, toks, fw), F32),
             pltpu.VMEM((n_row, tile_rows, BLK, BLK), BF16),
             pltpu.VMEM((n_row, tile_rows, BLK, BLK), BF16),
-            pltpu.VMEM((2, n_chip) + piece, F32),
+            pltpu.VMEM((2, 2) + piece, F32),
+            pltpu.VMEM((2,) + piece, F32),
             pltpu.VMEM((2, n_chip) + piece, BF16),
             pltpu.VMEM((2, n_chip) + piece, BF16),
             pltpu.VMEM((2, n_chip) + piece, BF16),
@@ -515,7 +541,8 @@
             dma((2, 2, half, SUBS)),
             dma((2, 2, half, SUBS)),
             dma((2, 2, half, SUBS)),
-            dma((2, 2)),
+            dma((2, n_x)),
+            dma((2, n_x)),
             dma((2, max(n_x - 1, 1))),
             dma((2, max(n_x - 1, 1))),
             dma((2, 2)),

time: 116 us -> 113 us (0.974)
  Pallas kernels: 112 us -> 109 us
    pallas_call x1, Pallas kernels: 112 us -> 109 us  [shards(): pl.pallas_call(functools.partial(kernel, n_row, n_col, tile_rows, n_block...]
where the time goes in v3:
time: 113 us
  Pallas kernels  109 us (96%)
  local copies, waits for them, and re-layouts  2.8 us (2%)
    pallas_call x1, Pallas kernels, shards(): pl.pallas_call(functools.partial(kernel, n_row, n_col, tile_rows, n_block...  109 us
    unnamed x4, local copies, waits for them, and re-layouts  2.8 us

profile of v3, /device:TPU:1, one launch (start us, length us, event | category | flops | bytes accessed | tf_op | source)
XLA Modules:
  0.0 112.5 jit_solution(1465755334787914833)
XLA Ops:
  0.6 109.1 %ffn.1 = (bf16[24,512]{1,0:T(8,128)(2,1)S(1)}, bf16[24,512]{1,0:T(8,128)(2,1)S(1)}, f32[8,128,128]{2,1,0:T(8,128)S(1)}, f32[8,128,128]{2,1,0:T(8,128)S(1)}) custom-call(bf16[24,512]{1,0:T(8,128)(2,1)} %tok_ref.1, bf16[24,512]{1,0:T(8,128)(2,1)} %cot_ref.1, s32[2,16]{1,0:T(2,128)} %bitcast.2, s32[2,16]{1,0:T(2,128)} %bitcast.3, bf16[16,128,128]{2,1,0:T(8,128)(2,1)} %w1_hbm.1, ...), custom_call_target="tpu_custom_call" | custom-call | tf_op jit(solution)/shard_map/ffn/pallas_call | solution.py:504
  109.7 0.6 copy.14
  110.3 0.6 copy.15
  111.0 0.8 copy.16
  111.7 0.8 copy.17

commit v4 on v3

--- a/solution.py
+++ b/solution.py
@@ -261,17 +261,25 @@
                 def _(s=s, way=way, j=j):
                     ag_copy(ph, way, j, t, s).start()
 
-    def consume(ph, j):
+    def use_sum(ph, j):
         if ph == 0:
             acc[0] += mm(ag0[j], w2d[j], NN)
+        else:
+            acc[1] += mm(ag1[j], w1d[j], NT)
+
+    def use_grad(ph, j):
+        if ph == 0:
             grad = mm(ag0[j], xp[1], TN)
             for a in range(tile_rows):
                 g2d[j, a] = grad[:, a * BLK : (a + 1) * BLK].astype(BF16)
         else:
-            acc[1] += mm(ag1[j], w1d[j], NT)
             grad = mm(xt[...], ag1[j], NN)
             for a in range(tile_rows):
                 g1d[j, a] = grad[a * BLK : (a + 1) * BLK, :].astype(BF16)
+
+    def consume(ph, j):
+        use_sum(ph, j)
+        use_grad(ph, j)
 
     def ag_use(ph, t):
         consume(ph, origin(0, t))
@@ -408,6 +416,43 @@
 
         lax.fori_loop(0, own_blocks, one, 0)
 
+    def sent_gathers(ph):
+        for way in range(2):
+            for s in range(SUBS):
+
+                def one(t, carry, way=way, s=s):
+                    ag_copy(ph, way, z, t, s).wait_send()
+                    return carry
+
+                lax.fori_loop(0, half if long_way(way, s) else half - 1, one, 0)
+
+    def sent_first():
+        for ph in range(2):
+            for q in range(1, n_col):
+                x_copy(ph, q).wait_send()
+            for way in range(2):
+                for s in range(SUBS):
+
+                    def one(t, carry, ph=ph, way=way, s=s):
+                        rs_copy(ph, way, t + 1, s).wait_send()
+                        return carry
+
+                    lax.fori_loop(0, half if long_way(way, s) else half - 1, one, 0)
+        sent_gathers(0)
+
+    def sent_results(ph):
+        for dx in range(n_x):
+            y1_copy(ph, dx).wait_send()
+        for dx in range(1, n_x):
+            y2_copy(ph, dx).wait_send()
+        y3_copy(ph).wait_send()
+
+        def one(m, carry):
+            w_copy(ph, m).wait_send()
+            return carry
+
+        lax.fori_loop(0, own_blocks, one, 0)
+
     dense1()
     x_start(1)
     for s in range(SUBS):
@@ -440,42 +485,23 @@
 
     lax.fori_loop(LAG, 2 * half + LAG, both, 0)
     y2(0)
+    sent_first()
     ag_pass(1, half)
-    ag_use(1, half)
+    last_block = origin(0, half)
+    use_sum(1, last_block)
     y1(1)
+    use_grad(1, last_block)
     send_weights(1)
+    sent_gathers(1)
     y3(0)
     y2(1)
     y4(0, out_ref)
     sum_weights(0, gw2_ref)
+    sent_results(0)
     y3(1)
     sum_weights(1, gw1_ref)
     y4(1, gt_ref)
-
-    for ph in range(2):
-        for q in range(1, n_col):
-            x_copy(ph, q).wait_send()
-        for dx in range(n_x):
-            y1_copy(ph, dx).wait_send()
-        for dx in range(1, n_x):
-            y2_copy(ph, dx).wait_send()
-        y3_copy(ph).wait_send()
-
-        def sent_weights(m, carry, ph=ph):
-            w_copy(ph, m).wait_send()
-            return carry
-
-        lax.fori_loop(0, own_blocks, sent_weights, 0)
-        for way in range(2):
-            for s in range(SUBS):
-                hops = half if long_way(way, s) else half - 1
-
-                def sent_rows(t, carry, ph=ph, way=way, s=s):
-                    rs_copy(ph, way, t + 1, s).wait_send()
-                    ag_copy(ph, way, z, t, s).wait_send()
-                    return carry
-
-                lax.fori_loop(0, hops, sent_rows, 0)
+    sent_results(1)
 
 
 def shards(n_row, n_col, tokens, cotangent, w1_blocks, w1_index, w2_blocks, w2_index):

time: 113 us -> 113 us (level)
  no operation moved by 1% of the time
where the time goes in v4:
time: 113 us; the launch traced here: 112 us
  Pallas kernels  108 us (96%)
  local copies, waits for them, and re-layouts  2.8 us (2%)
    pallas_call x1, Pallas kernels, shards(): pl.pallas_call(functools.partial(kernel, n_row, n_col, tile_rows, n_block...  108 us
    unnamed x4, local copies, waits for them, and re-layouts  2.8 us

profile of v4, /device:TPU:1, one launch (start us, length us, event | category | flops | bytes accessed | tf_op | source)
XLA Modules:
  0.0 111.8 jit_solution(17558636807218085)
XLA Ops:
  0.6 108.4 %ffn.1 = (bf16[24,512]{1,0:T(8,128)(2,1)S(1)}, bf16[24,512]{1,0:T(8,128)(2,1)S(1)}, f32[8,128,128]{2,1,0:T(8,128)S(1)}, f32[8,128,128]{2,1,0:T(8,128)S(1)}) custom-call(bf16[24,512]{1,0:T(8,128)(2,1)} %tok_ref.1, bf16[24,512]{1,0:T(8,128)(2,1)} %cot_ref.1, s32[2,16]{1,0:T(2,128)} %bitcast.2, s32[2,16]{1,0:T(2,128)} %bitcast.3, bf16[16,128,128]{2,1,0:T(8,128)(2,1)} %w1_hbm.1, ...), custom_call_target="tpu_custom_call" | custom-call | tf_op jit(solution)/shard_map/ffn/pallas_call | solution.py:530
  109.0 0.6 copy.14
  109.6 0.6 copy.15
  110.2 0.8 copy.16
  111.0 0.8 copy.17

commit v5 on v4

--- a/solution.py
+++ b/solution.py
@@ -227,13 +227,16 @@
                 tanh = jnp.tanh(C0 * (total + C1 * (total * total * total)))
                 value = 0.5 * total * (1.0 + tanh)
             else:
+                value = total * hid[sub(s)]
+            ag[ph][z, sub(s)] = value.astype(BF16)
+            for way in range(2):
+                ag_copy(ph, way, z, 0, s).start()
+        if ph == 0:
+            for s in range(SUBS):
                 v = hid[sub(s)]
                 tanh = jnp.tanh(C0 * (v + C1 * (v * v * v)))
                 slope = 0.5 * (1.0 + tanh) + 0.5 * v * (1.0 - tanh * tanh) * (C0 * (1.0 + 3.0 * C1 * (v * v)))
-                value = total * slope
-            ag[ph][z, sub(s)] = value.astype(BF16)
-            for way in range(2):
-                ag_copy(ph, way, z, 0, s).start()
+                hid[sub(s)] = slope
 
     def origin(way, t):
         return lax.rem(z + n_row - t, n_row) if way == 0 else lax.rem(z + t, n_row)

time: 113 us -> 113 us (level)
  no operation moved by 1% of the time
where the time goes in v5:
time: 113 us; the launch traced here: 112 us
  Pallas kernels  108 us (96%)
  local copies, waits for them, and re-layouts  2.8 us (2%)
    pallas_call x1, Pallas kernels, shards(): pl.pallas_call(functools.partial(kernel, n_row, n_col, tile_rows, n_block...  108 us
    unnamed x4, local copies, waits for them, and re-layouts  2.8 us

profile of v5, /device:TPU:1, one launch (start us, length us, event | category | flops | bytes accessed | tf_op | source)
XLA Modules:
  0.0 111.8 jit_solution(2082321774466661909)
XLA Ops:
  0.6 108.3 %ffn.1 = (bf16[24,512]{1,0:T(8,128)(2,1)S(1)}, bf16[24,512]{1,0:T(8,128)(2,1)S(1)}, f32[8,128,128]{2,1,0:T(8,128)S(1)}, f32[8,128,128]{2,1,0:T(8,128)S(1)}) custom-call(bf16[24,512]{1,0:T(8,128)(2,1)} %tok_ref.1, bf16[24,512]{1,0:T(8,128)(2,1)} %cot_ref.1, s32[2,16]{1,0:T(2,128)} %bitcast.2, s32[2,16]{1,0:T(2,128)} %bitcast.3, bf16[16,128,128]{2,1,0:T(8,128)(2,1)} %w1_hbm.1, ...), custom_call_target="tpu_custom_call" | custom-call | tf_op jit(solution)/shard_map/ffn/pallas_call | solution.py:533
  109.0 0.6 copy.14
  109.6 0.6 copy.15
  110.2 0.8 copy.16
  111.0 0.8 copy.17
